TPU v7x, 32 devices: a whole 2x2x4 slice. The times are simulated.
32 devices in a mesh: dp: 8 (over z, y), tensor: 4 (over x, core).
Axes of the slice: x: 2, y: 2, z: 4, core: 2. Of those that a mesh axis runs over, the one named last changes fastest.
Arguments:
- tokens: bfloat16 [32768, 384], P('dp'), may hold values from -6 to 6
- crop_ids: int32 [32768], P('dp'), may hold values from 0 to 5, as said below
- cotangent: bfloat16 [32768, 384], P('dp'), may hold values from -18 to 18
- key_tokens: bfloat16 [32768, 384], P('dp'), may hold values from -6 to 6
- entry_weight: float32 [384, 3, 384], P('dp', None, 'tensor'), may hold values from -0.15625 to 0.15625
- exit_weight: float32 [384, 384], P('tensor', 'dp'), may hold values from -2.5 to 2.5
- up_weight: float32 [384, 1536], P('dp', 'tensor'), may hold values from -0.3125 to 0.3125
- down_weight: float32 [1536, 384], P('tensor', 'dp'), may hold values from -0.15625 to 0.15625
- small_params: float32 [6, 384], P(None, 'dp'), may hold values from -1.5 to 7
- hidden_bias: float32 [1536], P(('tensor', 'dp')), may hold values from -2.5 to 2.5
- entry_first: float32 [384, 3, 384], P('dp', None, 'tensor'), may hold values from -0.00048828125 to 0.00048828125
- exit_first: float32 [384, 384], P('tensor', 'dp'), may hold values from -0.00012207031 to 0.00012207031
- up_first: float32 [384, 1536], P('dp', 'tensor'), may hold values from -0.00048828125 to 0.00048828125
- down_first: float32 [1536, 384], P('tensor', 'dp'), may hold values from -0.00048828125 to 0.00048828125
- small_first: float32 [6, 384], P(None, 'dp'), may hold values from -0.0008544922 to 0.0008544922
- hidden_first: float32 [1536], P(('tensor', 'dp')), may hold values from -0.00010681152 to 0.00010681152
- entry_second: float32 [384, 3, 384], P('dp', None, 'tensor'), may hold values from 5.639166e-10 to 2.2556663e-09
- exit_second: float32 [384, 384], P('tensor', 'dp'), may hold values from 3.3834994e-11 to 1.3533998e-10
- up_second: float32 [384, 1536], P('dp', 'tensor'), may hold values from 5.639166e-10 to 2.2556663e-09
- down_second: float32 [1536, 384], P('tensor', 'dp'), may hold values from 5.639166e-10 to 2.2556663e-09
- small_second: float32 [6, 384], P(None, 'dp'), may hold values from 1.6917496e-09 to 6.7669985e-09
- hidden_second: float32 [1536], P(('tensor', 'dp')), may hold values from 2.2556663e-11 to 9.022665e-11
- key_entry: bfloat16 [384, 3, 384], P(None, None, 'tensor'), may hold values from -0.15625 to 0.15625
- key_exit: bfloat16 [384, 384], P('tensor'), may hold values from -2.5 to 2.5
- key_up: bfloat16 [384, 1536], P(None, 'tensor'), may hold values from -0.3125 to 0.3125
- key_down: bfloat16 [1536, 384], P('tensor'), may hold values from -0.15625 to 0.15625
- key_small: bfloat16 [6, 384], replicated, may hold values from -1.5 to 7
- key_hidden: bfloat16 [1536], P('tensor'), may hold values from -2.5 to 2.5
Outputs:
- block_output: bfloat16 [32768, 384], P('dp')
- key_output: bfloat16 [32768, 384], P('dp')
- input_grad: bfloat16 [32768, 384], P('dp')
- grad_norm: float32 [], replicated
- entry_moment: float32 [384, 3, 384], P('dp', None, 'tensor')
- entry_square: float32 [384, 3, 384], P('dp', None, 'tensor')
- entry_master: float32 [384, 3, 384], P('dp', None, 'tensor')
- exit_moment: float32 [384, 384], P('tensor', 'dp')
- exit_square: float32 [384, 384], P('tensor', 'dp')
- exit_master: float32 [384, 384], P('tensor', 'dp')
- up_moment: float32 [384, 1536], P('dp', 'tensor')
- up_square: float32 [384, 1536], P('dp', 'tensor')
- up_master: float32 [384, 1536], P('dp', 'tensor')
- down_moment: float32 [1536, 384], P('tensor', 'dp')
- down_square: float32 [1536, 384], P('tensor', 'dp')
- down_master: float32 [1536, 384], P('tensor', 'dp')
- small_moment: float32 [6, 384], P(None, 'dp')
- small_square: float32 [6, 384], P(None, 'dp')
- small_master: float32 [6, 384], P(None, 'dp')
- hidden_moment: float32 [1536], P(('tensor', 'dp'))
- hidden_square: float32 [1536], P(('tensor', 'dp'))
- hidden_master: float32 [1536], P(('tensor', 'dp'))
Inputs may be any that keep to these rules, and one draw needn't show every extreme that they name: `crop_ids`: each aligned block of 512 rows holds whole crops of 197 or 101 rows from its first row on, numbered 0, 1, 2 and so on in order; the rows after them carry 5 and are padding.
All inputs are finite; a program needn't handle non-finite values.
Results may differ from a plain program's by a relative error of at most 0.017.
The roundings to bfloat16 on the way count: a program that leaves them out, or rounds other values in their place, can miss the bound.
Values may be sent and summed in bfloat16 or wider, within the bound.
A program may use at most 192 MiB of HBM per device.

v0:
```python
from functools import partial

import jax
import jax.numpy as jnp
from jax import lax
from jax.sharding import PartitionSpec as P

HEAD_DIM = 32
PACK = 512
CROPS = 5
STEP = 10


LN_EPS = 1e-06
CLIP = 1.0
RATE_MATRIX = 0.03
RATE_EXIT = 0.2
RATE_SMALL = 0.5
RATE_BIAS = 0.3
BETA_ONE = 0.9
BETA_TWO = 0.999
ADAM_EPS = 1e-08
DECAY = 0.05
MASKED = -1e30


def normalize(values, gain, shift):
    mean = jnp.mean(values, axis=1, keepdims=True)
    centred = values - mean
    spread = jnp.mean(centred * centred, axis=1, keepdims=True)
    scale = lax.rsqrt(spread + LN_EPS)
    unit = centred * scale
    return (unit * gain + shift, unit, scale)


def normalize_back(grad, unit, scale, gain):
    scaled = grad * gain
    first = jnp.mean(scaled, axis=1, keepdims=True)
    second = jnp.mean(scaled * unit, axis=1, keepdims=True)
    back = scale * (scaled - first - unit * second)
    return (back, jnp.sum(grad * unit, axis=0), jnp.sum(grad, axis=0))


def masked_scores(packed, segment):
    scores = jnp.einsum(
        "qhd,khd->hqk", packed[:, 0], packed[:, 1], preferred_element_type=jnp.float32
    ) * HEAD_DIM ** (-0.5)
    same = segment[:, None] == segment[None, :]
    return jnp.where(same[None], scores, MASKED)


def attend(packed, segment):
    scores = masked_scores(packed, segment)
    top = jnp.max(scores, axis=2, keepdims=True)
    expo = jnp.exp(scores - top)
    total = jnp.sum(expo, axis=2, keepdims=True)
    probs = (expo / total).astype(jnp.bfloat16)
    mixed = jnp.einsum("hqk,khd->qhd", probs, packed[:, 2], preferred_element_type=jnp.float32)
    return (mixed.astype(jnp.bfloat16), top + jnp.log(total))


def attend_back(packed, segment, logsum, grad_mixed):
    scores = masked_scores(packed, segment)
    probs = jnp.exp(scores - logsum)
    grad_values = jnp.einsum(
        "hqk,qhd->khd", probs.astype(jnp.bfloat16), grad_mixed, preferred_element_type=jnp.float32
    )
    grad_probs = jnp.einsum(
        "qhd,khd->hqk", grad_mixed, packed[:, 2], preferred_element_type=jnp.float32
    )
    inner = jnp.sum(probs * grad_probs, axis=2, keepdims=True)
    grad_scores = (probs * (grad_probs - inner)).astype(jnp.bfloat16)
    scale = HEAD_DIM ** (-0.5)
    grad_query = (
        jnp.einsum("hqk,khd->qhd", grad_scores, packed[:, 1], preferred_element_type=jnp.float32)
        * scale
    )
    grad_keys = (
        jnp.einsum("hqk,qhd->khd", grad_scores, packed[:, 0], preferred_element_type=jnp.float32)
        * scale
    )
    return jnp.stack([grad_query, grad_keys, grad_values], axis=1).astype(jnp.bfloat16)


def forward(inputs, segments, weights):
    entry_work, exit_work, upper_work, lower_work, small_work, bias_work = weights
    rows = inputs.shape[0]
    width = exit_work.shape[0]
    first_norm, first_unit, first_scale = normalize(inputs, small_work[0], small_work[1])
    first_norm = first_norm.astype(jnp.bfloat16)
    entry_flat = entry_work.reshape(entry_work.shape[0], -1)
    packed = jnp.dot(first_norm, entry_flat, preferred_element_type=jnp.float32).astype(
        jnp.bfloat16
    )
    packed = packed.reshape(-1, PACK, 3, width // HEAD_DIM, HEAD_DIM)
    blocks = segments.reshape(-1, PACK)
    attended, logsum = lax.map(lambda item: attend(item[0], item[1]), (packed, blocks))
    attended = attended.reshape(rows, width)
    branch = jnp.dot(attended, exit_work, preferred_element_type=jnp.float32)
    middle = inputs + lax.psum(branch, "tensor") + small_work[4]
    second_norm, second_unit, second_scale = normalize(middle, small_work[2], small_work[3])
    second_norm = second_norm.astype(jnp.bfloat16)
    preact = jnp.dot(second_norm, upper_work, preferred_element_type=jnp.float32) + bias_work
    activated = jax.nn.gelu(preact, approximate=False).astype(jnp.bfloat16)
    product = jnp.dot(activated, lower_work, preferred_element_type=jnp.float32)
    result = (
        middle
        + lax.psum(product.astype(jnp.bfloat16), "tensor").astype(jnp.float32)
        + small_work[5]
    ).astype(jnp.bfloat16)
    kept = (
        first_norm,
        first_unit,
        first_scale,
        packed,
        blocks,
        logsum,
        attended,
        second_norm,
        second_unit,
        second_scale,
        preact,
        activated,
    )
    return (result, kept)


def backward(grad_out, weights, kept):
    entry_work, exit_work, upper_work, lower_work, small_work, bias_work = weights
    (
        first_norm,
        first_unit,
        first_scale,
        packed,
        blocks,
        logsum,
        attended,
        second_norm,
        second_unit,
        second_scale,
        preact,
        activated,
    ) = kept
    rows = grad_out.shape[0]
    width = exit_work.shape[0]
    grad_low = grad_out.astype(jnp.bfloat16)
    grad_act = jnp.dot(grad_low, lower_work.T, preferred_element_type=jnp.float32)
    gelu_pull = jax.vjp(partial(jax.nn.gelu, approximate=False), preact)[1]
    grad_pre = gelu_pull(grad_act)[0].astype(jnp.bfloat16)
    grad_lower = jnp.dot(activated.T, grad_low, preferred_element_type=jnp.float32)
    grad_upper = jnp.dot(second_norm.T, grad_pre, preferred_element_type=jnp.float32)
    grad_bias = jnp.sum(grad_pre.astype(jnp.float32), axis=0)
    second_partial = jnp.dot(grad_pre, upper_work.T, preferred_element_type=jnp.float32)
    grad_second = lax.psum(second_partial, "tensor")
    middle_back, grad_gain_two, grad_shift_two = normalize_back(
        grad_second, second_unit, second_scale, small_work[2]
    )
    grad_middle = grad_out + middle_back
    middle_low = grad_middle.astype(jnp.bfloat16)
    grad_exit = jnp.dot(attended.T, middle_low, preferred_element_type=jnp.float32)
    grad_mixed = jnp.dot(middle_low, exit_work.T, preferred_element_type=jnp.float32).astype(
        jnp.bfloat16
    )
    grad_mixed = grad_mixed.reshape(-1, PACK, width // HEAD_DIM, HEAD_DIM)
    grad_packed = lax.map(
        lambda item: attend_back(item[0], item[1], item[2], item[3]),
        (packed, blocks, logsum, grad_mixed),
    )
    grad_packed = grad_packed.reshape(rows, -1)
    entry_flat = entry_work.reshape(entry_work.shape[0], -1)
    grad_entry = jnp.dot(first_norm.T, grad_packed, preferred_element_type=jnp.float32).reshape(
        entry_work.shape
    )
    first_partial = jnp.dot(grad_packed, entry_flat.T, preferred_element_type=jnp.float32)
    grad_first = lax.psum(first_partial.astype(jnp.bfloat16), "tensor").astype(jnp.float32)
    input_back, grad_gain_one, grad_shift_one = normalize_back(
        grad_first, first_unit, first_scale, small_work[0]
    )
    grad_inputs = (grad_middle + input_back).astype(jnp.bfloat16)
    grad_small = jnp.stack(
        [
            grad_gain_one,
            grad_shift_one,
            grad_gain_two,
            grad_shift_two,
            jnp.sum(grad_middle, axis=0),
            jnp.sum(grad_out, axis=0),
        ]
    )
    return ((grad_entry, grad_exit, grad_upper, grad_lower, grad_small, grad_bias), grad_inputs)


def sum_squares(grads, copies):
    total = jnp.sum(grads[4] * grads[4]) / copies
    for grad in (grads[0], grads[1], grads[2], grads[3], grads[5]):
        total = total + jnp.sum(grad * grad)
    return total


def adamw(grad, first, second, master, decay, rate):
    moment = BETA_ONE * first + (1.0 - BETA_ONE) * grad
    square = BETA_TWO * second + (1.0 - BETA_TWO) * grad * grad
    ahead = moment / (1.0 - BETA_ONE**STEP)
    spread = square / (1.0 - BETA_TWO**STEP)
    return (
        moment,
        square,
        master - rate * (ahead / (jnp.sqrt(spread) + ADAM_EPS) + decay * master),
    )


def on_device(
    tokens,
    crop_ids,
    cotangent,
    key_tokens,
    entry_weight,
    exit_weight,
    up_weight,
    down_weight,
    small_params,
    hidden_bias,
    entry_first,
    exit_first,
    up_first,
    down_first,
    small_first,
    hidden_first,
    entry_second,
    exit_second,
    up_second,
    down_second,
    small_second,
    hidden_second,
    key_entry,
    key_exit,
    key_up,
    key_down,
    key_small,
    key_hidden,
):
    gathered = (
        lax.all_gather(entry_weight.astype(jnp.bfloat16), "dp", axis=0, tiled=True),
        lax.all_gather(exit_weight.astype(jnp.bfloat16), "dp", axis=1, tiled=True),
        lax.all_gather(up_weight.astype(jnp.bfloat16), "dp", axis=0, tiled=True),
        lax.all_gather(down_weight.astype(jnp.bfloat16), "dp", axis=1, tiled=True),
        lax.all_gather(small_params.astype(jnp.bfloat16), "dp", axis=1, tiled=True),
        lax.all_gather(hidden_bias.astype(jnp.bfloat16), "dp", axis=0, tiled=True),
    )
    working = (
        gathered[0],
        gathered[1],
        gathered[2],
        gathered[3],
        gathered[4].astype(jnp.float32),
        gathered[5].astype(jnp.float32),
    )
    valid = (crop_ids < CROPS).astype(jnp.float32)[:, None]
    result, kept = forward(tokens.astype(jnp.float32), crop_ids, working)
    grads, grad_inputs = backward(cotangent.astype(jnp.float32) * valid, working, kept)
    key_weights = (
        key_entry,
        key_exit,
        key_up,
        key_down,
        key_small.astype(jnp.float32),
        key_hidden.astype(jnp.float32),
    )
    key_result, unused = forward(key_tokens.astype(jnp.float32), crop_ids, key_weights)
    copies = float(lax.axis_size("tensor"))
    total = lax.psum((grads[0], grads[1], grads[2], grads[3], grads[4], grads[5]), "dp")
    squares = lax.psum(sum_squares(total, copies), "tensor")
    index = lax.axis_index("dp")
    count = lax.axis_size("dp")
    shares = tuple(
        (
            lax.dynamic_slice_in_dim(
                grad, index * (grad.shape[along] // count), grad.shape[along] // count, along
            )
            for grad, along in zip(total, (0, 1, 0, 1, 1, 0))
        )
    )
    norm_value = jnp.sqrt(squares)
    factor = CLIP / jnp.maximum(norm_value, CLIP)
    entry_new = adamw(
        shares[0] * factor, entry_first, entry_second, entry_weight, DECAY, RATE_MATRIX
    )
    exit_new = adamw(shares[1] * factor, exit_first, exit_second, exit_weight, DECAY, RATE_EXIT)
    upper_new = adamw(shares[2] * factor, up_first, up_second, up_weight, DECAY, RATE_MATRIX)
    lower_new = adamw(shares[3] * factor, down_first, down_second, down_weight, DECAY, RATE_MATRIX)
    small_new = adamw(shares[4] * factor, small_first, small_second, small_params, 0.0, RATE_SMALL)
    bias_new = adamw(shares[5] * factor, hidden_first, hidden_second, hidden_bias, 0.0, RATE_BIAS)
    return (
        result,
        key_result,
        grad_inputs,
        norm_value,
        entry_new[0],
        entry_new[1],
        entry_new[2],
        exit_new[0],
        exit_new[1],
        exit_new[2],
        upper_new[0],
        upper_new[1],
        upper_new[2],
        lower_new[0],
        lower_new[1],
        lower_new[2],
        small_new[0],
        small_new[1],
        small_new[2],
        bias_new[0],
        bias_new[1],
        bias_new[2],
    )


def solution(mesh):
    return jax.shard_map(
        on_device,
        mesh=mesh,
        in_specs=(
            P("dp", None),
            P("dp"),
            P("dp", None),
            P("dp", None),
            P("dp", None, "tensor"),
            P("tensor", "dp"),
            P("dp", "tensor"),
            P("tensor", "dp"),
            P(None, "dp"),
            P(("tensor", "dp")),
            P("dp", None, "tensor"),
            P("tensor", "dp"),
            P("dp", "tensor"),
            P("tensor", "dp"),
            P(None, "dp"),
            P(("tensor", "dp")),
            P("dp", None, "tensor"),
            P("tensor", "dp"),
            P("dp", "tensor"),
            P("tensor", "dp"),
            P(None, "dp"),
            P(("tensor", "dp")),
            P(None, None, "tensor"),
            P("tensor", None),
            P(None, "tensor"),
            P("tensor", None),
            P(),
            P("tensor"),
        ),
        out_specs=(
            P("dp", None),
            P("dp", None),
            P("dp", None),
            P(),
            P("dp", None, "tensor"),
            P("dp", None, "tensor"),
            P("dp", None, "tensor"),
            P("tensor", "dp"),
            P("tensor", "dp"),
            P("tensor", "dp"),
            P("dp", "tensor"),
            P("dp", "tensor"),
            P("dp", "tensor"),
            P("tensor", "dp"),
            P("tensor", "dp"),
            P("tensor", "dp"),
            P(None, "dp"),
            P(None, "dp"),
            P(None, "dp"),
            P(("tensor", "dp")),
            P(("tensor", "dp")),
            P(("tensor", "dp")),
        ),
        check_vma=False,
    )
```

profile of v0, /device:TPU:0, one launch (start us, length us, event | category | flops | bytes accessed | tf_op | source)
XLA Modules:
  0.0 1085.4 jit_solution(12029710641603105077)
XLA Ops:
  9.6 27.8 %all-gather = bf16[8,48,6]{1,2,0:T(8,128)(2,1)S(1)} all-gather(bf16[1,48,6]{1,2,0:T(8,128)(2,1)S(1)} %convert_bitcast_fusion), channel_id=1, replica_groups=mesh['dp'=8,'tensor'=4] {'dp'}, dimensions={0}, use_global_device_ids=true | all-gather | bytes 5184 | tf_op jit(solution)/shard_map/all_gather | solution.py:247
  45.6 30.7 %all_gather.20 = bf16[96,384]{0,1:T(8,128)(2,1)S(1)} all-gather(bf16[96,48]{0,1:T(8,128)(2,1)S(1)} %copy-done.46), channel_id=1, replica_groups=mesh['dp'=8,'tensor'=4] {'dp'}, dimensions={1}, use_global_device_ids=true | all-gather | bytes 82944 | tf_op jit(solution)/shard_map/all_gather | solution.py:244
  76.3 32.8 %all_gather.19 = bf16[384,3,96]{2,0,1:T(8,128)(2,1)} all-gather(bf16[48,3,96]{2,0,1:T(8,128)(2,1)S(1)} %convert_element_type.144), channel_id=1, replica_groups=mesh['dp'=8,'tensor'=4] {'dp'}, dimensions={0}, use_global_device_ids=true | all-gather | bytes 248832 | tf_op jit(solution)/shard_map/all_gather | solution.py:243
  116.6 33.2 %while.32 = (s32[]{:T(128)}, bf16[8,512,3,32]{1,3,2,0:T(8,128)(2,1)S(1)}, f32[8,3,512,1]{2,1,3,0:T(4,128)}, bf16[8,512,3,3,32]{1,4,3,2,0:T(8,128)(2,1)S(1)}, s32[8,512]{1,0:T(8,128)}, /*index=5*/s32[]{:T(128)}) while((s32[]{:T(128)}, bf16[8,512,3,32]{1,3,2,0:T(8,128)(2,1)S(1)}, f32[8,3,512,1]{2,1,3,0:T(4,128)}, ...), condition=%wide.region_5.6_spmd, body=%wide.region_2.5_spmd.sunk | while | flops 110410240 | bytes 11530333 | solution.py:97
  166.1 87.3 %while.33 = (s32[]{:T(128)}, bf16[8,512,3,32]{1,3,2,0:T(8,128)(2,1)}, bf16[8,512,3,3,32]{1,4,3,2,0:T(8,128)(2,1)}, s32[8,512]{1,0:T(8,128)}, s32[]{:T(128)}) while((s32[]{:T(128)}, bf16[8,512,3,32]{1,3,2,0:T(8,128)(2,1)}, bf16[8,512,3,3,32]{1,4,3,2,0:T(8,128)(2,1)}, s32[8,512]{1,0:T(8,128)}, s32[]{:T(128)}) %tuple.128), condition=%wide.region_15.16_spmd, body=%wide.region_12.15_spmd.sunk | while | flops 105693696 | bytes 7819345 | solution.py:97
  258.4 20.9 %all-reduce = bf16[384]{0:T(512)(128)(2,1)} all-reduce(bf16[384]{0:T(512)(128)(2,1)} %dynamic-update-slice), channel_id=1, replica_groups=mesh['dp'=8,'tensor'=4] {'dp'}, use_global_device_ids=true, to_apply=%add | all-reduce | flops 384 | bytes 1536
  284.1 33.0 %all_gather.23 = bf16[384,384]{0,1:T(8,128)(2,1)} all-gather(bf16[384,48]{0,1:T(8,128)(2,1)S(1)} %convert_element_type.152), channel_id=1, replica_groups=mesh['dp'=8,'tensor'=4] {'dp'}, dimensions={1}, use_global_device_ids=true | all-gather | bytes 331776 | tf_op jit(solution)/shard_map/all_gather | solution.py:246
  317.1 33.0 %all_gather.21 = bf16[384,384]{1,0:T(8,128)(2,1)} all-gather(bf16[48,384]{1,0:T(8,128)(2,1)S(1)} %convert_element_type.148), channel_id=1, replica_groups=mesh['dp'=8,'tensor'=4] {'dp'}, dimensions={0}, use_global_device_ids=true | all-gather | bytes 331776 | tf_op jit(solution)/shard_map/all_gather | solution.py:245
  363.8 17.3 %multiply_convert_fusion.1 = (bf16[4096,384]{1,0:T(8,128)(2,1)}, f32[4096,384]{1,0:T(8,128)S(1)}, f32[4096,384]{1,0:T(8,128)}) fusion(f32[384]{0:T(512)S(1)} %copy-done.67, bf16[4096,384]{1,0:T(8,128)(2,1)S(1)} %add_convert_fusion.4, bf16[384,384]{1,0:T(8,128)(2,1)S(1)} %copy-done.23), kind=kOutput, calls=%fused_computation.133 | convolution fusion | flops 1311768576 | bytes 19170816 | tf_op jit(solution)/shard_map/dot_general | solution.py:103
  381.2 7.4 convert_reduce_fusion.3
  390.2 4.8 fusion.158
  397.0 7.3 convolution_convert_fusion.2
  410.7 202.5 %all-reduce.14.cloned.1.call-done = (f32[4096,384]{1,0:T(8,128)}, f32[4096,384]{1,0:T(8,128)}) async-done(((f32[4096,384]{1,0:T(8,128)}, f32[4096,384]{1,0:T(8,128)}), (f32[4096,384]{1,0:T(8,128)}, f32[4096,384]{1,0:T(8,128)})) %all-reduce.14.cloned.1.call-update) | async-done | bytes 12582928 | tf_op jit(solution)/shard_map/psum | solution.py:100
  617.8 10.5 multiply_reduce_fusion.1
  638.2 74.8 %while.34 = (s32[]{:T(128)}, bf16[8,512,3,3,32]{1,4,3,2,0:T(8,128)(2,1)}, bf16[8,512,3,3,32]{1,4,3,2,0:T(8,128)(2,1)}, s32[8,512]{1,0:T(8,128)}, f32[8,3,512,1]{...) while((s32[]{:T(128)}, bf16[8,512,3,3,32]{1,4,3,2,0:T(8,128)(2,1)}, ...), condition=%wide.region_25.26_spmd, body=%wide.region_23.25_spmd.sunk | while | flops 260127232 | bytes 26318956 | solution.py:165
  722.7 21.2 %convolution_convert_fusion.1 = bf16[4096,384]{1,0:T(8,128)(2,1)} fusion(bf16[384,384]{1,0:T(8,128)(2,1)S(1)} %copy-done, bf16[384,384]{1,0:T(8,128)(2,1)} %param.58, f32[384]{0:T(512)S(1)} %copy-done.66, f32[384]{0:T(512)S(1)} %copy-done.69, f32[384]{0:T(512)S(1)} %copy-done.70, f32[4096]{0:T(1024)S(1)} %add_rsqrt_fusion, f32[4096]{0:T(1024)S(1)} %copy-done.41, ...), kind=kOutput, calls=%fused_computation.154 | convolution fusion | flops 2533883904 | bytes 13211648 | tf_op jit(solution)/shard_map/dot_general | solution.py:105
  743.9 5.5 convolution_convert_fusion
  750.1 72.3 %all-reduce.12.cloned.1.call-done = (f32[384,3,96]{2,0,1:T(8,128)}, f32[96,384]{0,1:T(8,128)}, f32[384,384]{1,0:T(8,128)}, f32[384,384]{0,1:T(8,128)}) async-done(((f32[384,3,96]{2,0,1:T(8,128)}, f32[96,384]{0,1:T(8,128)}, f32[384,384]{1,0:T(8,128)}, f32[384,384]{0,1:T(8,128)}), (f32[384,3,96]{2,0,1:T(8,128)}, f32[96,384]{0,1:T(8,128)}, f32[384,384]{1,0:T(8,128)}, ...) | async-done | bytes 1769488 | tf_op jit(solution)/shard_map/psum | solution.py:271
  829.5 166.6 %all-reduce.16.cloned.1.call-done = (bf16[4096,384]{1,0:T(8,128)(2,1)}, bf16[4096,384]{1,0:T(8,128)(2,1)}, bf16[4096,384]{1,0:T(8,128)(2,1)}) async-done(((bf16[4096,384]{1,0:T(8,128)(2,1)}, bf16[4096,384]{1,0:T(8,128)(2,1)}, bf16[4096,384]{1,0:T(8,128)(2,1)}), (bf16[4096,384]{1,0:T(8,128)(2,1)}, bf16[4096,384]{1,0:T(8,128)(2,1)}, bf16[4096,384]{1,0:T(8,128)(2,1)})) %all-reduce.16.cloned.1.call-update) | async-done | bytes 9437200 | tf_op jit(solution)/shard_map/psum | solution.py:108
  996.1 5.8 fusion.69
  1001.9 37.1 %all-reduce.1 = (f32[6,384]{1,0:T(8,128)S(1)}, f32[384]{0:T(512)S(1)}) all-reduce(f32[6,384]{1,0:T(8,128)S(1)} %stack.39, f32[384]{0:T(512)S(1)} %copy-done.65), channel_id=1, replica_groups=mesh['dp'=8,'tensor'=4] {'dp'}, use_global_device_ids=true, to_apply=%region_35.36 | all-reduce | flops 2688 | bytes 21504 | tf_op jit(solution)/shard_map/psum | solution.py:271
  1044.1 6.5 psum.103
  1051.4 7.8 add_convert_fusion.1
  1070.1 7.1 fusion.60
  (443 shorter events, 305.1 us)
Async XLA Ops:
  7.2 715.5 %copy-start = (bf16[384,384]{1,0:T(8,128)(2,1)S(1)}, bf16[384,384]{1,0:T(8,128)(2,1)}, u32[]{:S(2)}) copy-start(bf16[384,384]{1,0:T(8,128)(2,1)} %param.59) | copy-start | bytes 884740
  7.2 103.7 %copy-start.4 = (bf16[4096,384]{1,0:T(8,128)(2,1)S(1)}, bf16[4096,384]{1,0:T(8,128)(2,1)}, u32[]{:S(2)}) copy-start(bf16[4096,384]{1,0:T(8,128)(2,1)} %param.34) | copy-start | bytes 9437188
  7.2 38.4 %copy-start.24 = (f32[48,3,96]{2,0,1:T(8,128)S(1)}, f32[48,3,96]{2,0,1:T(8,128)}, u32[]{:S(2)}) copy-start(f32[48,3,96]{2,0,1:T(8,128)} %param.38) | copy-start | bytes 165892
  7.2 348.0 %all-reduce.10.cloned.1.call-start = ((), (), s32[]{:S(2)}) async-start(), calls=%async_computation | async-start | bytes 12582912 | tf_op jit(solution)/shard_map/psum | solution.py:100
  41.9 72.7 %copy-start.28 = (f32[4096]{0:T(1024)}, f32[4096]{0:T(1024)S(1)}, u32[]{:S(2)}) copy-start(f32[4096]{0:T(1024)S(1)} %broadcast_multiply_fusion.7) | copy-start | bytes 49156
  155.8 457.4 %all-reduce.14.cloned.1.call-start = ((), (), s32[]{:S(2)}) async-start(), calls=%async_computation.2 | async-start | bytes 25165824 | tf_op jit(solution)/shard_map/psum | solution.py:100
  166.1 184.1 %copy-start.42 = (s32[4096]{0:T(1024)S(1)}, s32[4096]{0:T(1024)}, u32[]{:S(2)}) copy-start(s32[4096]{0:T(1024)} %param.35) | copy-start | bytes 49156
  361.4 19.8 %copy-start.30 = (f32[4096]{0:T(1024)}, f32[4096]{0:T(1024)S(1)}, u32[]{:S(2)}) copy-start(f32[4096]{0:T(1024)S(1)} %add_rsqrt_fusion.2) | copy-start | bytes 49156
  363.8 17.4 %copy-start.15 = (bf16[4096,384]{1,0:T(8,128)(2,1)}, bf16[4096,384]{1,0:T(8,128)(2,1)S(1)}, u32[]{:S(2)}) copy-start(bf16[4096,384]{1,0:T(8,128)(2,1)S(1)} %add_convert_fusion.4) | copy-start | bytes 9437188
  363.8 17.4 %copy-start.17 = (bf16[4096,384]{1,0:T(8,128)(2,1)S(1)}, bf16[4096,384]{1,0:T(8,128)(2,1)}, u32[]{:S(2)}) copy-start(bf16[4096,384]{1,0:T(8,128)(2,1)} %param.36) | copy-start | bytes 9437188
  363.8 17.4 %copy-start.22 = (bf16[384,384]{0,1:T(8,128)(2,1)S(1)}, bf16[384,384]{0,1:T(8,128)(2,1)}, u32[]{:S(2)}) copy-start(bf16[384,384]{0,1:T(8,128)(2,1)} %all_gather.23) | copy-start | bytes 884740
  363.8 17.4 %copy-start.43 = (f32[4096]{0:T(1024)S(1)}, f32[4096]{0:T(1024)}, u32[]{:S(2)}) copy-start(f32[4096]{0:T(1024)} %compare_convert_fusion) | copy-start | bytes 49156
  395.1 427.4 %all-reduce.12.cloned.1.call-start = ((), (), s32[]{:S(2)}) async-start(), calls=%async_computation.1 | async-start | bytes 3932160 | tf_op jit(solution)/shard_map/psum | solution.py:271
  613.2 15.2 %slice-start = ((s8[6291456]{0:T(1024)(128)(4,1)}), s8[2097152]{0:T(1024)(128)(4,1)S(1)}, s32[]{:S(2)}) async-start(s8[6291456]{0:T(1024)(128)(4,1)} %bitcast.223), calls=%async_computation.4 | async-start | bytes 4194304
  613.2 15.2 %slice-start.4 = ((s8[6291456]{0:T(1024)(128)(4,1)}), s8[4194304]{0:T(1024)(128)(4,1)S(1)}, s32[]{:S(2)}) async-start(s8[6291456]{0:T(1024)(128)(4,1)} %bitcast.227), calls=%async_computation.8 | async-start | bytes 8388608
  617.1 11.3 %copy-start.40 = (f32[4096]{0:T(1024)}, f32[4096]{0:T(1024)S(1)}, u32[]{:S(2)}) copy-start(f32[4096]{0:T(1024)S(1)} %broadcast_multiply_fusion.4) | copy-start | bytes 49156
  617.8 10.6 slice-start.5
  617.8 10.6 copy-start.19
  722.6 273.4 %all-reduce.16.cloned.1.call-start = ((), (), s32[]{:S(2)}) async-start(), calls=%async_computation.3 | async-start | bytes 18874368 | tf_op jit(solution)/shard_map/psum | solution.py:108
  749.4 252.5 %copy-start.65 = (f32[384]{0:T(512)S(1)}, f32[384]{0:T(512)}, u32[]{:S(2)}) copy-start(f32[384]{0:T(512)} %get-tuple-element.327) | copy-start | bytes 4612
  749.4 301.9 %copy-start.59 = (f32[384]{0:T(512)S(1)}, f32[384]{0:T(512)}, u32[]{:S(2)}) copy-start(f32[384]{0:T(512)} %get-tuple-element.242) | copy-start | bytes 4612
  996.1 63.1 %slice-start.2 = ((s8[6291456]{0:T(1024)(128)(4,1)}), s8[2097152]{0:T(1024)(128)(4,1)S(1)}, s32[]{:S(2)}) async-start(s8[6291456]{0:T(1024)(128)(4,1)} %bitcast.225), calls=%async_computation.6 | async-start | bytes 4194304
  1059.4 10.7 copy-start.6
  1059.4 10.7 copy-start.8
  (61 other events, 308.7 us)
Sparse Core Ops, SparseCore 0:
  155.9 118.9 all-reduce.9
  395.2 217.9 all-reduce.13
  722.8 99.6 all-reduce.11
  825.8 170.2 all-reduce.15
where the time goes:
time: 1100 us; the launch traced here: 1090 us
  waiting for transfers between devices  441 us (40%)
  blocking collectives  222 us (20%)
  matrix products  208 us (19%)
  other arithmetic  118 us (11%)
  local copies, waits for them, and re-layouts  73.6 us (7%)
  between operations  21.8 us (2%)
    psum x2, waiting for transfers between devices, forward(): middle = inputs + lax.psum(branch, 'tensor') + small_work[4]  202 us
    psum x1, waiting for transfers between devices, forward(): lax.psum(product.astype(jnp.bfloat16), 'tensor').astype(jnp.float32)  167 us
    psum x1, waiting for transfers between devices, on_device(): lax.psum((grads[0], grads[1], grads[2], grads[3], grads[4], grads[5]), 'dp')  72.3 us
    psum x1, blocking collectives, on_device(): lax.psum((grads[0], grads[1], grads[2], grads[3], grads[4], grads[5]), 'dp')  37.1 us
    sub x8, matrix products, attend(): expo = jnp.exp(scores - top)  37 us
    all_gather x1, blocking collectives, on_device(): lax.all_gather(up_weight.astype(jnp.bfloat16), 'dp', axis=0, tiled=True)  33 us
    all_gather x1, blocking collectives, on_device(): lax.all_gather(down_weight.astype(jnp.bfloat16), 'dp', axis=1, tiled=True)  33 us
    all_gather x1, blocking collectives, on_device(): lax.all_gather(entry_weight.astype(jnp.bfloat16), 'dp', axis=0, tiled=True)  32.8 us
  transfers between devices with their start and end apart: 4, of which 3 were waited for; matrix products, arithmetic and copies ran while one was open for 15% of the time, Pallas kernels for 0%

commit v1 on v0

v1 whole, which is shorter than its diff:
```python
import math
from functools import partial

import jax
import jax.numpy as jnp
from jax import lax
from jax.experimental import pallas as pl
from jax.experimental.pallas import tpu as pltpu
from jax.sharding import PartitionSpec as P

HEAD_DIM = 32
PACK = 512
CROPS = 5
STEP = 10
LN_EPS = 1e-06
CLIP = 1.0
RATE_MATRIX = 0.03
RATE_EXIT = 0.2
RATE_SMALL = 0.5
RATE_BIAS = 0.3
BETA_ONE = 0.9
BETA_TWO = 0.999
ADAM_EPS = 1e-08
DECAY = 0.05
MASKED = -1e30

SCALE = HEAD_DIM ** (-0.5)
EXP_SCALE = SCALE * math.log2(math.e)
LANES = 128
HEADS_HERE = 3
USED = HEADS_HERE * HEAD_DIM
ONES = USED + CROPS + 1
ATT = 4 * LANES
SMALL_AT = USED
HIDDEN_AT = USED + 6
MESH = pl.DeviceIdType.MESH
BF = jnp.bfloat16
F32 = jnp.float32
VMEM = pltpu.VMEM
NT = (((1,), (1,)), ((), ()))
TN = (((0,), (0,)), ((), ()))

TAIL_AT = 0.305
TAIL = (
    0.12163973599672318,
    0.12246678024530411,
    0.10342107713222504,
    0.12102094292640686,
    -0.03797539696097374,
    0.18571528792381287,
    -0.15298734605312347,
    0.036698948591947556,
)


def mm(left, right):
    return jnp.dot(left, right, preferred_element_type=F32)


def mm_nt(left, right):
    return lax.dot_general(left, right, NT, preferred_element_type=F32)


def norm_parts(values):
    mean = jnp.mean(values, axis=1, keepdims=True)
    centred = values - mean
    spread = jnp.mean(centred * centred, axis=1, keepdims=True)
    scale = lax.rsqrt(spread + LN_EPS)
    return (centred * scale, scale)


def norm_back(grad, unit, scale, gain):
    scaled = grad * gain
    first = jnp.mean(scaled, axis=1, keepdims=True)
    second = jnp.mean(scaled * unit, axis=1, keepdims=True)
    return scale * (scaled - first - unit * second)


def tail_parts(pre):
    size = jnp.abs(pre)
    base = 1.0 + TAIL_AT * size
    part = pl.reciprocal(base, approx=True)
    part = part * (2.0 - base * part)
    poly = TAIL[7]
    for k in range(6, -1, -1):
        poly = poly * part + TAIL[k]
    bell = jnp.exp(-0.5 * pre * pre)
    tail = poly * part * bell
    return (jnp.where(pre < 0.0, tail, 1.0 - tail), bell)


def small_rows(w_ref):
    rows = w_ref[0, :, 0:LANES].astype(F32).T
    return rows[SMALL_AT : SMALL_AT + 6]


def hidden_row(w_ref, t):
    return w_ref[t, :, 0:LANES].astype(F32).T[HIDDEN_AT : HIDDEN_AT + 1]


def id_lanes(ids):
    place = lax.broadcasted_iota(jnp.int32, (LANES, PACK), 0)
    match = (place - USED) == ids
    ones = (place >= ONES) & (place < ONES + 3)
    key_side = jnp.where(match | ones, 1.0, 0.0).T
    crop = (place >= USED) & (place < ONES)
    query_side = jnp.where(crop & jnp.logical_not(match), MASKED, 0.0).astype(BF)
    return (key_side, query_side)


def attention(qkv_ref, a_ref, lse_ref, base, query_side, groups):
    place = lax.broadcasted_iota(jnp.int32, (LANES, PACK), 0) // HEAD_DIM
    ones = jnp.ones((16, PACK), BF)
    blank = jnp.zeros((LANES - USED, PACK), F32)
    rows = pl.ds(base, PACK)
    for g in range(groups):
        at = g * 3 * LANES
        query = qkv_ref[rows, at : at + LANES].T
        keys = qkv_ref[rows, at + LANES : at + 2 * LANES]
        values = qkv_ref[rows, at + 2 * LANES : at + 3 * LANES].T
        outs = []
        for h in range(HEADS_HERE):
            scores = mm(keys, jnp.where(place == h, query, query_side))
            top = jnp.max(scores, axis=0, keepdims=True)
            probs = jnp.exp2((scores - top) * EXP_SCALE).astype(BF)
            mix = jnp.concatenate([values[h * HEAD_DIM : (h + 1) * HEAD_DIM], ones], axis=0)
            mixed = mm(mix, probs)
            total = mixed[HEAD_DIM : HEAD_DIM + 1]
            outs.append(mixed[:HEAD_DIM] * (1.0 / total))
            if lse_ref is not None:
                line = g * HEADS_HERE + h
                lse_ref[line : line + 1, rows] = top + jnp.log(total) * (1.0 / SCALE)
        a_ref[rows, g * LANES : (g + 1) * LANES] = (
            jnp.concatenate(outs + [blank], axis=0).T.astype(BF)
        )


def forward_front(x_ref, ids_ref, w_ref, small, qkv_ref, a_ref, h1_ref, x1_ref, lse_ref, base, pack):
    groups = w_ref.shape[0]
    rows = pl.ds(base, PACK)
    values = x_ref[rows, :].astype(F32)
    unit, _ = norm_parts(values)
    first = (unit * small[0:1] + small[1:2]).astype(BF)
    if h1_ref is not None:
        h1_ref[rows, :] = first
    key_side, query_side = id_lanes(ids_ref[pack])
    for g in range(groups):
        at = g * 3 * LANES
        qkv_ref[rows, at : at + LANES] = mm(first, w_ref[g, :, 0:LANES]).astype(BF)
        packed = mm(first, w_ref[g, :, LANES : 3 * LANES])
        qkv_ref[rows, at + LANES : at + 2 * LANES] = (packed[:, :LANES] + key_side).astype(BF)
        qkv_ref[rows, at + 2 * LANES : at + 3 * LANES] = (packed[:, LANES:] + key_side).astype(BF)
    attention(qkv_ref, a_ref, lse_ref, base, query_side, groups)
    branch = mm_nt(a_ref[rows, 0:LANES], w_ref[0, :, 3 * LANES : 4 * LANES])
    for g in range(1, groups):
        branch += mm_nt(
            a_ref[rows, g * LANES : (g + 1) * LANES], w_ref[g, :, 3 * LANES : 4 * LANES]
        )
    x1_ref[rows, :] = x_ref[rows, :].astype(F32) + branch + small[4:5]


def ffn_tile(w_ref, j):
    depth = w_ref.shape[1]
    per = depth // LANES
    up, down = [], []
    for b in (2 * j, 2 * j + 1):
        t, o = b // per, (b % per) * LANES
        up.append(w_ref[t, :, ATT + o : ATT + o + LANES])
        down.append(w_ref[t, :, ATT + depth + o : ATT + depth + o + LANES])
    return (jnp.concatenate(up, axis=1), jnp.concatenate(down, axis=1))


def key_kernel(place_ref, x_ref, ids_ref, w_ref, out_ref, qkv_ref, a_ref, x1_ref, h2_ref, bias_ref):
    rows_here, depth = x_ref.shape
    small = small_rows(w_ref)
    for t in range(w_ref.shape[0]):
        bias_ref[:, t * depth : (t + 1) * depth] = hidden_row(w_ref, t)

    @pl.loop(0, rows_here // PACK)
    def _(pack):
        base = pl.multiple_of(pack * PACK, PACK)
        forward_front(x_ref, ids_ref, w_ref, small, qkv_ref, a_ref, None, x1_ref, None, base, pack)
        rows = pl.ds(base, PACK)
        unit, _ = norm_parts(x1_ref[rows, :])
        h2_ref[rows, :] = (unit * small[2:3] + small[3:4]).astype(BF)

    tiles = w_ref.shape[0] * depth // (2 * LANES)
    step = 256

    @pl.loop(0, rows_here // step)
    def _(r):
        rows = pl.ds(pl.multiple_of(r * step, step), step)
        second = h2_ref[rows, :]
        total = x1_ref[rows, :] + small[5:6]
        for j in range(tiles):
            up, down = ffn_tile(w_ref, j)
            pre = mm(second, up) + bias_ref[:, j * 256 : (j + 1) * 256]
            acts = []
            for i in range(0, step, 64):
                piece = pre[i : i + 64]
                phi, _ = tail_parts(piece)
                acts.append((piece * phi).astype(BF))
            total += mm_nt(jnp.concatenate(acts, axis=0), down)
        out_ref[rows, :] = total.astype(BF)


def query_kernel(
    place_ref,
    x_ref,
    cot_ref,
    ids_ref,
    w_ref,
    out_ref,
    qkv_ref,
    a_ref,
    lse_ref,
    h1_ref,
    dx1_ref,
    grad_ref,
    line_ref,
    hidden_ref,
    x1_ref,
    h2_ref,
    h2t_ref,
    eb_ref,
    ebt_ref,
    act_ref,
    dpre_ref,
    dh2_ref,
    bias_ref,
):
    rows_here, depth = x_ref.shape
    groups = w_ref.shape[0]
    small = small_rows(w_ref)
    for t in range(groups):
        bias_ref[:, t * depth : (t + 1) * depth] = hidden_row(w_ref, t)

    lse_ref[...] = jnp.zeros_like(lse_ref)
    h2t_ref[depth:, :] = jnp.ones((h2t_ref.shape[0] - depth, rows_here), BF)

    @pl.loop(0, rows_here // PACK)
    def _(pack):
        base = pl.multiple_of(pack * PACK, PACK)
        forward_front(
            x_ref, ids_ref, w_ref, small, qkv_ref, a_ref, h1_ref, x1_ref, lse_ref, base, pack
        )
        rows = pl.ds(base, PACK)
        unit, _ = norm_parts(x1_ref[rows, :])
        second = (unit * small[2:3] + small[3:4]).astype(BF)
        h2_ref[rows, :] = second
        h2t_ref[0:depth, rows] = second.T
        valid = jnp.where(ids_ref[pack] < CROPS, 1.0, 0.0)
        valid = jnp.broadcast_to(valid, (LANES, PACK)).T[:, 0:1]
        low = (cot_ref[rows, :].astype(F32) * valid).astype(BF)
        eb_ref[rows, :] = low
        ebt_ref[:, rows] = low.T

    tiles = groups * depth // (2 * LANES)
    step = 256
    chunks = rows_here // step
    per = depth // LANES
    for j in range(tiles):
        up, down = ffn_tile(w_ref, j)
        bias = bias_ref[:, j * 256 : (j + 1) * 256]
        for r in range(chunks):
            rows = slice(r * step, (r + 1) * step)
            pre = mm(h2_ref[rows, :], up) + bias
            da = mm(eb_ref[rows, :], down)
            acts, dps = [], []
            for i in range(0, step, 64):
                piece = pre[i : i + 64]
                phi, bell = tail_parts(piece)
                acts.append((piece * phi).astype(BF))
                slope = phi + piece * (bell * (1.0 / math.sqrt(2.0 * math.pi)))
                dps.append((da[i : i + 64] * slope).astype(BF))
            act = jnp.concatenate(acts, axis=0)
            dpre = jnp.concatenate(dps, axis=0)
            act_ref[rows, :] = act
            dpre_ref[rows, :] = dpre
            if j == 0:
                x1_now = x1_ref[rows, :] + small[5:6]
                qsum = x1_now + mm_nt(act, down)
                dsum = mm_nt(dpre, up)
            else:
                qsum = dh2_ref[0, rows, :] + mm_nt(act, down)
                dsum = dh2_ref[1, rows, :] + mm_nt(dpre, up)
            dh2_ref[0, rows, :] = qsum
            dh2_ref[1, rows, :] = dsum
        gup = mm(h2t_ref[...], dpre_ref[...])
        gdown = mm(ebt_ref[...], act_ref[...])
        for k, b in enumerate((2 * j, 2 * j + 1)):
            t, o = b // per, (b % per) * LANES
            grad_ref[t, :, o : o + LANES] = gup[:depth, k * LANES : (k + 1) * LANES].astype(BF)
            grad_ref[t, :, depth + o : depth + o + LANES] = gdown[
                :, k * LANES : (k + 1) * LANES
            ].astype(BF)
            hidden_ref[t : t + 1, o : o + LANES] = gup[
                depth : depth + 1, k * LANES : (k + 1) * LANES
            ]

    out_ref[...] = dh2_ref[0].astype(BF)

    line_ref[...] = jnp.zeros_like(line_ref)

    @pl.loop(0, rows_here // PACK)
    def _(pack):
        rows = pl.ds(pl.multiple_of(pack * PACK, PACK), PACK)
        unit, scale = norm_parts(x1_ref[rows, :])
        grad = dh2_ref[1, rows, :]
        valid = jnp.where(ids_ref[pack] < CROPS, 1.0, 0.0)
        valid = jnp.broadcast_to(valid, (LANES, PACK)).T[:, 0:1]
        wide = cot_ref[rows, :].astype(F32) * valid
        dx1 = wide + norm_back(grad, unit, scale, small[2:3])
        dx1_ref[rows, :] = dx1
        line_ref[2:3, :] += jnp.sum(grad * unit, axis=0, keepdims=True)
        line_ref[3:4, :] += jnp.sum(grad, axis=0, keepdims=True)
        line_ref[4:5, :] += jnp.sum(dx1, axis=0, keepdims=True)
        line_ref[5:6, :] += jnp.sum(wide, axis=0, keepdims=True)


def attention_back(qkv_ref, a_ref, lse_ref, da_ref, dqkv_ref, base, query_side, groups):
    place = lax.broadcasted_iota(jnp.int32, (LANES, PACK), 0)
    head_of = place // HEAD_DIM
    lane = lax.broadcasted_iota(jnp.int32, (PACK, LANES), 1) // HEAD_DIM
    rows = pl.ds(base, PACK)
    none = jnp.zeros((PACK, LANES), BF)

    def split(line):
        high = line.astype(BF).astype(F32)
        rest = line - high
        middle = rest.astype(BF).astype(F32)
        low = rest - middle
        block = jnp.where(
            place == ONES,
            high,
            jnp.where(place == ONES + 1, middle, jnp.where(place == ONES + 2, low, 0.0)),
        )
        return block.astype(BF)

    for g in range(groups):
        at = g * 3 * LANES
        query = qkv_ref[rows, at : at + LANES]
        keys = qkv_ref[rows, at + LANES : at + 2 * LANES]
        values = qkv_ref[rows, at + 2 * LANES : at + 3 * LANES]
        grad = da_ref[rows, g * LANES : (g + 1) * LANES]
        query_t, keys_t, grad_t = query.T, keys.T, grad.T
        both = a_ref[rows, g * LANES : (g + 1) * LANES].T.astype(F32) * grad_t.astype(F32)
        dq, dk, dv = [], None, None
        for h in range(HEADS_HERE):
            part = slice(h * HEAD_DIM, (h + 1) * HEAD_DIM)
            line = g * HEADS_HERE + h
            lse = lse_ref[line : line + 1, rows]
            side = jnp.where(place < ONES, query_side, split(-lse))
            scores = mm(keys, jnp.where(head_of == h, query_t, side))
            probs = jnp.exp2(scores * EXP_SCALE)
            inner = jnp.sum(both[part], axis=0, keepdims=True)
            pull = mm(values, jnp.where(head_of == h, grad_t, split(-inner)))
            low = probs.astype(BF)
            dscores = (probs * pull).astype(BF)
            dv_h = mm(low, jnp.where(lane == h, grad, none))
            dk_h = mm(dscores, jnp.where(lane == h, query, none))
            dv = dv_h if dv is None else dv + dv_h
            dk = dk_h if dk is None else dk + dk_h
            dq.append(mm(keys_t[part], dscores))
        dq.append(jnp.zeros((LANES - USED, PACK), F32))
        dqkv_ref[rows, at : at + LANES] = (jnp.concatenate(dq, axis=0).T * SCALE).astype(BF)
        dqkv_ref[rows, at + LANES : at + 2 * LANES] = (dk * SCALE).astype(BF)
        dqkv_ref[rows, at + 2 * LANES : at + 3 * LANES] = dv.astype(BF)


def back_kernel(
    place_ref,
    x_ref,
    ids_ref,
    w_ref,
    qkv_ref,
    a_ref,
    lse_ref,
    h1_ref,
    dx1_ref,
    line_ref,
    hidden_ref,
    out_ref,
    grad_ref,
    da_ref,
    dqkv_ref,
    h1t_ref,
    dybt_ref,
    sums_ref,
):
    rows_here, depth = x_ref.shape
    groups = w_ref.shape[0]
    small = small_rows(w_ref)
    sums_ref[...] = jnp.zeros_like(sums_ref)
    sums_ref[SMALL_AT : SMALL_AT + 8, :] = line_ref[...]

    @pl.loop(0, rows_here // PACK)
    def _(pack):
        base = pl.multiple_of(pack * PACK, PACK)
        rows = pl.ds(base, PACK)
        _, query_side = id_lanes(ids_ref[pack])
        low = dx1_ref[rows, :].astype(BF)
        dybt_ref[:, rows] = low.T
        h1t_ref[:, rows] = h1_ref[rows, :].T
        for g in range(groups):
            da_ref[rows, g * LANES : (g + 1) * LANES] = mm(
                low, w_ref[g, :, 3 * LANES : 4 * LANES]
            ).astype(BF)
        attention_back(qkv_ref, a_ref, lse_ref, da_ref, dqkv_ref, base, query_side, groups)
        width = 3 * LANES
        grad = mm_nt(dqkv_ref[rows, 0:width], w_ref[0, :, 0:width])
        for g in range(1, groups):
            grad += mm_nt(dqkv_ref[rows, g * width : (g + 1) * width], w_ref[g, :, 0:width])
        unit, scale = norm_parts(x_ref[rows, :].astype(F32))
        back = norm_back(grad, unit, scale, small[0:1])
        out_ref[rows, :] = (dx1_ref[rows, :] + back).astype(BF)
        sums_ref[SMALL_AT : SMALL_AT + 1, :] += jnp.sum(grad * unit, axis=0, keepdims=True)
        sums_ref[SMALL_AT + 1 : SMALL_AT + 2, :] += jnp.sum(grad, axis=0, keepdims=True)

    lane = lax.broadcasted_iota(jnp.int32, (depth, LANES), 1)
    for g in range(groups):
        width = 3 * LANES
        sums_ref[HIDDEN_AT : HIDDEN_AT + 1, :] = hidden_ref[g : g + 1, :]
        extra = sums_ref[...].T
        entry = mm(h1t_ref[...], dqkv_ref[:, g * width : (g + 1) * width])
        grad_ref[g, :, 0:LANES] = jnp.where(lane < USED, entry[:, :LANES], extra).astype(BF)
        grad_ref[g, :, LANES:width] = entry[:, LANES:].astype(BF)
        grad_ref[g, :, width : width + LANES] = mm(
            dybt_ref[...], a_ref[:, g * LANES : (g + 1) * LANES]
        ).astype(BF)


def params():
    return pltpu.CompilerParams(vmem_limit_bytes=60 * 2**20)


def whole(shape):
    return pl.BlockSpec(shape, lambda i, place: (0,) * len(shape))


def own_rows(rows, depth):
    return pl.BlockSpec((rows, depth), lambda i, place: (place[0], 0))


def own_ids(packs):
    return pl.BlockSpec((packs, 1, PACK), lambda i, place: (place[0], 0, 0))


def run_key(place, tokens, ids, weights, rows):
    depth = tokens.shape[1]
    groups, _, width = weights.shape
    return pl.pallas_call(
        key_kernel,
        grid_spec=pltpu.PrefetchScalarGridSpec(
            num_scalar_prefetch=1,
            grid=(1,),
            in_specs=[own_rows(rows, depth), own_ids(rows // PACK), whole(weights.shape)],
            out_specs=whole((rows, depth)),
            scratch_shapes=[
                VMEM((rows, groups * 3 * LANES), BF),
                VMEM((rows, groups * LANES), BF),
                VMEM((rows, depth), F32),
                VMEM((rows, depth), BF),
                VMEM((1, groups * depth), F32),
            ],
        ),
        out_shape=jax.ShapeDtypeStruct((rows, depth), BF),
        compiler_params=params(),
        name="key_block",
    )(place, tokens, ids, weights)


def run_query(place, tokens, cotangent, ids, weights, rows):
    depth = tokens.shape[1]
    groups = weights.shape[0]
    outs = [
        ((rows, depth), BF),
        ((rows, groups * 3 * LANES), BF),
        ((rows, groups * LANES), BF),
        ((16, rows), F32),
        ((rows, depth), BF),
        ((rows, depth), F32),
        ((groups, depth, 2 * depth), BF),
        ((8, depth), F32),
        ((groups, depth), F32),
    ]
    return pl.pallas_call(
        query_kernel,
        grid_spec=pltpu.PrefetchScalarGridSpec(
            num_scalar_prefetch=1,
            grid=(1,),
            in_specs=[
                own_rows(rows, depth),
                own_rows(rows, depth),
                own_ids(rows // PACK),
                whole(weights.shape),
            ],
            out_specs=[whole(shape) for shape, _ in outs],
            scratch_shapes=[
                VMEM((rows, depth), F32),
                VMEM((rows, depth), BF),
                VMEM((depth + 16, rows), BF),
                VMEM((rows, depth), BF),
                VMEM((depth, rows), BF),
                VMEM((rows, 2 * LANES), BF),
                VMEM((rows, 2 * LANES), BF),
                VMEM((2, rows, depth), F32),
                VMEM((1, groups * depth), F32),
            ],
        ),
        out_shape=[jax.ShapeDtypeStruct(shape, kind) for shape, kind in outs],
        compiler_params=params(),
        name="query_block",
    )(place, tokens, cotangent, ids, weights)


def run_back(place, tokens, ids, weights, kept, rows):
    depth = tokens.shape[1]
    groups = weights.shape[0]
    return pl.pallas_call(
        back_kernel,
        grid_spec=pltpu.PrefetchScalarGridSpec(
            num_scalar_prefetch=1,
            grid=(1,),
            in_specs=[own_rows(rows, depth), own_ids(rows // PACK), whole((groups, depth, ATT))]
            + [whole(item.shape) for item in kept],
            out_specs=[whole((rows, depth)), whole((groups, depth, ATT))],
            scratch_shapes=[
                VMEM((rows, groups * LANES), BF),
                VMEM((rows, groups * 3 * LANES), BF),
                VMEM((depth, rows), BF),
                VMEM((depth, rows), BF),
                VMEM((LANES, depth), F32),
            ],
        ),
        out_shape=[
            jax.ShapeDtypeStruct((rows, depth), BF),
            jax.ShapeDtypeStruct((groups, depth, ATT), BF),
        ],
        compiler_params=params(),
        name="back_block",
    )(place, tokens, ids, weights, *kept)


def pack_piece(entry, leave, up, down, small, hidden):
    def fill(block, *extra):
        block = jnp.concatenate([block] + [item.astype(block.dtype) for item in extra], axis=1)
        return jnp.pad(block, ((0, 0), (0, LANES - block.shape[1])))

    parts = [
        fill(entry[:, 0], small.T, hidden[:, None]),
        fill(entry[:, 1]),
        fill(entry[:, 2]),
        fill(leave.T),
        up,
        down.T,
    ]
    return jnp.concatenate([part.astype(BF) for part in parts], axis=1)


def unpack_piece(piece, depth):
    entry = jnp.stack([piece[:, k * LANES : k * LANES + USED] for k in range(3)], axis=1)
    leave = piece[:, 3 * LANES : 3 * LANES + USED].T
    up = piece[:, ATT : ATT + depth]
    down = piece[:, ATT + depth :].T
    small = piece[:, SMALL_AT : SMALL_AT + 6].T
    return (entry, leave, up, down, small, piece[:, HIDDEN_AT])


def adamw(grad, first, second, master, decay, rate):
    moment = BETA_ONE * first + (1.0 - BETA_ONE) * grad
    square = BETA_TWO * second + (1.0 - BETA_TWO) * grad * grad
    ahead = moment / (1.0 - BETA_ONE**STEP)
    spread = square / (1.0 - BETA_TWO**STEP)
    return (
        moment,
        square,
        master - rate * (ahead / (jnp.sqrt(spread) + ADAM_EPS) + decay * master),
    )


DECAYS = (DECAY, DECAY, DECAY, DECAY, 0.0, 0.0)
RATES = (RATE_MATRIX, RATE_EXIT, RATE_MATRIX, RATE_MATRIX, RATE_SMALL, RATE_BIAS)


def finish_plain(grad_att, grad_ffn, masters, firsts, seconds):
    depth = grad_att.shape[1]
    grads = jnp.concatenate([grad_att, grad_ffn], axis=2).astype(F32)
    own = lax.psum_scatter(grads, "tensor", scatter_dimension=0, tiled=False)
    own = lax.psum_scatter(own, "dp", scatter_dimension=0, tiled=True)
    shares = unpack_piece(own, depth)
    copies = float(lax.axis_size("tensor"))
    total = jnp.sum(shares[4] * shares[4]) / copies
    for k in (0, 1, 2, 3, 5):
        total = total + jnp.sum(shares[k] * shares[k])
    norm_value = jnp.sqrt(lax.psum(total, ("dp", "tensor")))
    factor = CLIP / jnp.maximum(norm_value, CLIP)
    outs = []
    for k in range(6):
        outs.extend(
            adamw(shares[k] * factor, firsts[k], seconds[k], masters[k], DECAYS[k], RATES[k])
        )
    return (norm_value, outs)


def on_device(*args):
    tokens, crop_ids, cotangent, key_tokens = args[:4]
    masters, firsts, seconds, keys = args[4:10], args[10:16], args[16:22], args[22:28]
    rows = tokens.shape[0] // lax.axis_size("tensor")
    place = lax.axis_index("tensor").astype(jnp.int32)[None]
    ids = crop_ids.reshape(-1, 1, PACK)
    key_weights = lax.all_gather(pack_piece(*keys), "tensor", axis=0)
    piece = pack_piece(*masters)
    weights = lax.all_gather(lax.all_gather(piece, "dp", axis=0, tiled=True), "tensor", axis=0)
    key_rows = run_key(place, key_tokens, ids, key_weights, rows)
    key_out = lax.all_gather(key_rows, "tensor", axis=0, tiled=True)
    forward = run_query(place, tokens, cotangent, ids, weights, rows)
    block_out = lax.all_gather(forward[0], "tensor", axis=0, tiled=True)
    qkv, a, lse, h1, dx1, grad_ffn, lines, hidden = forward[1:]
    grad_rows, grad_att = run_back(
        place, tokens, ids, weights, (qkv, a, lse, h1, dx1, lines, hidden), rows
    )
    input_grad = lax.all_gather(grad_rows, "tensor", axis=0, tiled=True)
    norm_value, outs = finish_plain(grad_att, grad_ffn, masters, firsts, seconds)
    return (block_out, key_out, input_grad, norm_value, *outs)


def solution(mesh):
    rows, line = P("dp", None), P("dp")
    entry, leave, up, down = P("dp", None, "tensor"), P("tensor", "dp"), P("dp", "tensor"), P("tensor", "dp")
    state = (entry, leave, up, down, P(None, "dp"), P(("tensor", "dp")))
    keys = (P(None, None, "tensor"), P("tensor", None), P(None, "tensor"), P("tensor", None), P(), P("tensor"))
    outs = tuple(spec for spec in state for _ in range(3))
    return jax.shard_map(
        on_device,
        mesh=mesh,
        in_specs=(rows, line, rows, rows) + state * 3 + keys,
        out_specs=(rows, rows, rows, P()) + outs,
        check_vma=False,
    )
```

time: 1100 us -> 493 us (0.45)
  matrix products: 208 us -> 0 us
  waiting for transfers between devices: 441 us -> 252 us
  blocking collectives: 222 us -> 75.7 us
  Pallas kernels: 0 us -> 94 us
  other arithmetic: 118 us -> 24.1 us
  local copies, waits for them, and re-layouts: 73.6 us -> 19.9 us
    psum x4 -> x0, waiting for transfers between devices: 441 us -> none  [the longest x2 202 us: forward(): middle = inputs + lax.psum(branch, 'tensor') + small_work[4]]
    dot_general x79 -> x0, matrix products: 171 us -> none  [the longest x16 31.8 us: attend(): jnp.einsum('hqk,khd->qhd', probs, packed[:, 2], preferred_element_type=jn...]
    reduce_scatter x0 -> x2, waiting for transfers between devices: none -> 136 us  [the longest x1 70.5 us: finish_plain(): own = lax.psum_scatter(own, 'dp', scatter_dimension=0, tiled=True)]
    all_gather x5 -> x1, blocking collectives: 157 us -> 36.4 us  [on_device(): lax.all_gather(piece, 'dp', axis=0, tiled=True)]
    all_gather x0 -> x5, waiting for transfers between devices: none -> 114 us  [the longest x1 35.1 us: on_device(): key_weights = lax.all_gather(pack_piece(*keys), 'tensor', axis=0)]
    pallas_call x0 -> x3, Pallas kernels: none -> 94 us  [the longest x1 39.8 us: run_query(): pl.pallas_call(query_kernel, grid_spec=pltpu.PrefetchScalarGridSpec(num_s...]
    reduce_sum x24 -> x5, other arithmetic: 52.3 us -> 6.42 us  [the longest x4 5 us: finish_plain(): total = total + jnp.sum(shares[k] * shares[k])]
    sub x8 -> x0, matrix products: 37 us -> none  [attend(): expo = jnp.exp(scores - top)]
  transfers between devices with their start and end apart: 4 -> 7, of which waited for: 3 -> 6; matrix products, arithmetic and copies ran while one was open for 15% -> 3% of each run, Pallas kernels for 0% -> 6%
where the time goes in v1:
time: 493 us; the launch traced here: 486 us
  waiting for transfers between devices  252 us (51%)
  Pallas kernels  94 us (19%)
  blocking collectives  75.7 us (15%)
  other arithmetic  24.1 us (5%)
  between operations  20.4 us (4%)
  local copies, waits for them, and re-layouts  19.9 us (4%)
    reduce_scatter x1, waiting for transfers between devices, finish_plain(): own = lax.psum_scatter(own, 'dp', scatter_dimension=0, tiled=True)  70.5 us
    reduce_scatter x1, waiting for transfers between devices, finish_plain(): own = lax.psum_scatter(grads, 'tensor', scatter_dimension=0, tiled=False)  65.6 us
    pallas_call x1, Pallas kernels, run_query(): pl.pallas_call(query_kernel, grid_spec=pltpu.PrefetchScalarGridSpec(num_s...  39.8 us
    psum x1, blocking collectives, finish_plain(): norm_value = jnp.sqrt(lax.psum(total, ('dp', 'tensor')))  39.3 us
    all_gather x1, blocking collectives, on_device(): lax.all_gather(piece, 'dp', axis=0, tiled=True)  36.4 us
    all_gather x1, waiting for transfers between devices, on_device(): key_weights = lax.all_gather(pack_piece(*keys), 'tensor', axis=0)  35.1 us
    all_gather x1, waiting for transfers between devices, on_device(): lax.all_gather(lax.all_gather(piece, 'dp', axis=0, tiled=True), 'tensor',...  34.2 us
    pallas_call x1, Pallas kernels, run_key(): pl.pallas_call(key_kernel, grid_spec=pltpu.PrefetchScalarGridSpec(num_sca...  27.3 us
  transfers between devices with their start and end apart: 7, of which 6 were waited for; matrix products, arithmetic and copies ran while one was open for 3% of the time, Pallas kernels for 6%

profile of v1, /device:TPU:0, one launch (start us, length us, event | category | flops | bytes accessed | tf_op | source)
XLA Modules:
  0.0 486.2 jit_solution(17130075395340274982)
XLA Ops:
  12.5 36.4 %all_gather.24 = bf16[384,1280]{1,0:T(8,128)(2,1)} all-gather(bf16[48,1280]{1,0:T(8,128)(2,1)S(1)} %bitcast_dynamic-update-slice_fusion.1), channel_id=1, replica_groups=mesh['dp'=8,'tensor'=4] {'dp'}, dimensions={0}, use_global_device_ids=true | all-gather | bytes 1105920 | tf_op jit(solution)/shard_map/all_gather | solution.py:614
  48.9 34.2 %all-gather.14.cloned.1.call-done = bf16[1536,1280]{1,0:T(8,128)(2,1)} async-done(((bf16[384,1280]{1,0:T(8,128)(2,1)}), bf16[1536,1280]{1,0:T(8,128)(2,1)}) %all-gather.14.cloned.1.call-update) | async-done | bytes 3932176 | tf_op jit(solution)/shard_map/all_gather | solution.py:614
  83.1 39.8 %query_block.1 = (bf16[1024,384]{1,0:T(8,128)(2,1)}, bf16[1024,1536]{1,0:T(8,128)(2,1)}, bf16[1024,512]{1,0:T(8,128)(2,1)}, f32[16,1024]{1,0:T(8,128)}, bf16[102...) custom-call(s32[1]{0:T(128)} %bitcast.place_ref, ...), custom_call_target="tpu_custom_call" | custom-call | tf_op jit(solution)/shard_map/query_block/pallas_call | solution.py:487
  122.9 26.9 %back_block.1 = (bf16[1024,384]{1,0:T(8,128)(2,1)}, bf16[4,384,512]{2,1,0:T(8,128)(2,1)}) custom-call(s32[1]{0:T(128)} %bitcast.place_ref, bf16[4096,384]{1,0:T(8,128)(2,1)} %x_ref.5, s32[8,1,512]{2,1,0:T(1,128)} %bitcast.61, bf16[4,384,1280]{2,1,0:T(8,128)(2,1)} %bitcast.57, bf16[1024,1536]{1,0:T(8,128)(2,1)} %get-tuple-element.34.qkv_ref, ...), custom_call_target="tpu_custom_call" | custom-call | tf_op jit(solution)/shard_map/back_block/pallas_call | solution.py:520
  149.8 5.1 %maximum_convert_fusion = f32[4,384,1280]{2,1,0:T(8,128)} fusion(bf16[4,384,768]{2,1,0:T(8,128)(2,1)S(1)} %copy-done.2, bf16[4,384,512]{2,1,0:T(8,128)(2,1)} %get-tuple-element.42), kind=kLoop, calls=%fused_computation | loop fusion | flops 7864320 | bytes 11796480 | tf_op jit(solution)/shard_map/convert_element_type | solution.py:588
  158.6 65.6 %reduce-scatter.3.cloned.1.call-done = f32[1,384,1280]{2,1,0:T(8,128)} async-done(((f32[4,384,1280]{2,1,0:T(8,128)}), f32[1,384,1280]{2,1,0:T(8,128)}) %reduce-scatter.3.cloned.1.call-update) | async-done | bytes 1966096 | tf_op jit(solution)/shard_map/reduce_scatter | solution.py:589
  224.2 35.1 %all-gather.16.cloned.1.call-done = bf16[1536,1280]{0,1:T(8,128)(2,1)} async-done(((bf16[384,1280]{0,1:T(8,128)(2,1)}), bf16[1536,1280]{0,1:T(8,128)(2,1)}) %all-gather.16.cloned.1.call-update) | async-done | bytes 3932176 | tf_op jit(solution)/shard_map/all_gather | solution.py:612
  259.4 6.4 %copy.81 = bf16[1536,1280]{1,0:T(8,128)(2,1)} copy(bf16[1536,1280]{0,1:T(8,128)(2,1)} %all-gather.16.cloned.1.call-done) | data formatting | bytes 7864320 | tf_op jit(solution)/shard_map/all_gather | solution.py:612
  265.9 27.3 %key_block.1 = bf16[1024,384]{1,0:T(8,128)(2,1)} custom-call(s32[1]{0:T(128)} %bitcast.place_ref, bf16[4096,384]{1,0:T(8,128)(2,1)} %x_ref.4, s32[8,1,512]{2,1,0:T(1,128)} %bitcast.62, bf16[4,384,1280]{2,1,0:T(8,128)(2,1)} %bitcast.58), custom_call_target="tpu_custom_call" | custom-call | tf_op jit(solution)/shard_map/key_block/pallas_call | solution.py:452
  293.7 25.8 %all-gather.8.cloned.1.call-done = bf16[4096,384]{1,0:T(8,128)(2,1)} async-done(((bf16[1024,384]{1,0:T(8,128)(2,1)}), bf16[4096,384]{1,0:T(8,128)(2,1)}) %all-gather.8.cloned.1.call-update) | async-done | bytes 3145744 | tf_op jit(solution)/shard_map/all_gather | solution.py:618
  319.5 70.5 %reduce-scatter.5.cloned.1.call-done = f32[48,1280]{1,0:T(8,128)} async-done(((f32[384,1280]{1,0:T(8,128)}), f32[48,1280]{1,0:T(8,128)}) %reduce-scatter.5.cloned.1.call-update) | async-done | bytes 245776 | tf_op jit(solution)/shard_map/reduce_scatter | solution.py:590
  390.0 1.4 multiply_reduce_fusion.6
  392.1 1.4 multiply_reduce_fusion.5
  395.4 1.5 multiply_reduce_fusion
  398.2 1.4 multiply_reduce_fusion.4
  400.3 19.3 %all-gather.10.cloned.1.call-done = bf16[4096,384]{1,0:T(8,128)(2,1)} async-done(((bf16[1024,384]{1,0:T(8,128)(2,1)}), bf16[4096,384]{1,0:T(8,128)(2,1)}) %all-gather.10.cloned.1.call-update) | async-done | bytes 3145744 | tf_op jit(solution)/shard_map/all_gather | solution.py:616
  419.7 39.3 %psum.7 = f32[]{:T(128)} all-reduce(f32[]{:T(128)S(6)} %add.131), channel_id=1, replica_groups=mesh['dp'=8,'tensor'=4] {'dp','tensor'}, use_global_device_ids=true, to_apply=%region_8.9 | all-reduce | flops 1 | bytes 8 | tf_op jit(solution)/shard_map/psum | solution.py:596
  464.7 1.6 multiply_subtract_fusion
  466.4 1.6 multiply_subtract_fusion.1
  468.0 1.4 multiply_subtract_fusion.4
  469.3 4.0 copy.103
  473.4 1.7 copy.104
  475.0 1.4 copy-done
  476.4 1.7 copy.105
  (106 shorter events, 15.0 us)
Async XLA Ops:
  7.2 75.9 %all-gather.14.cloned.1.call-start = ((), (), s32[]{:S(2)}) async-start(), calls=%async_computation.7 | async-start | bytes 4915200 | tf_op jit(solution)/shard_map/all_gather | solution.py:614
  48.9 175.3 %reduce-scatter.3.cloned.1.call-start = ((), (), s32[]{:S(2)}) async-start(), calls=%async_computation.5 | async-start | bytes 9830400 | tf_op jit(solution)/shard_map/reduce_scatter | solution.py:589
  155.0 104.4 %all-gather.16.cloned.1.call-start = ((), (), s32[]{:S(2)}) async-start(), calls=%async_computation.8 | async-start | bytes 4915200 | tf_op jit(solution)/shard_map/all_gather | solution.py:612
  157.4 136.3 %all-gather.12.cloned.1.call-start = ((), (), s32[]{:S(2)}) async-start(), calls=%async_computation.4 | async-start | bytes 3932160 | tf_op jit(solution)/shard_map/all_gather | solution.py:623
  158.0 161.5 %all-gather.8.cloned.1.call-start = ((), (), s32[]{:S(2)}) async-start(), calls=%async_computation.2 | async-start | bytes 3932160 | tf_op jit(solution)/shard_map/all_gather | solution.py:618
  158.6 231.4 %reduce-scatter.5.cloned.1.call-start = ((), (), s32[]{:S(2)}) async-start(), calls=%async_computation.6 | async-start | bytes 2211840 | tf_op jit(solution)/shard_map/reduce_scatter | solution.py:590
  224.2 195.5 %all-gather.10.cloned.1.call-start = ((), (), s32[]{:S(2)}) async-start(), calls=%async_computation.3 | async-start | bytes 3932160 | tf_op jit(solution)/shard_map/all_gather | solution.py:616
  265.8 27.7 %copy-start.22 = (f32[6,48]{1,0:T(8,128)S(1)}, f32[6,48]{1,0:T(8,128)}, u32[]{:S(2)}) copy-start(f32[6,48]{1,0:T(8,128)} %param.42) | copy-start | bytes 3460
  265.8 27.8 %copy-start.23 = (f32[6,48]{1,0:T(8,128)S(1)}, f32[6,48]{1,0:T(8,128)}, u32[]{:S(2)}) copy-start(f32[6,48]{1,0:T(8,128)} %param.48) | copy-start | bytes 3460
  265.8 196.8 %copy-start.4 = (f32[48,3,96]{2,0,1:T(8,128)S(1)}, f32[48,3,96]{2,0,1:T(8,128)}, u32[]{:S(2)}) copy-start(f32[48,3,96]{2,0,1:T(8,128)} %param.32) | copy-start | bytes 165892
  265.8 196.7 %copy-start.11 = (f32[48,3,96]{2,0,1:T(8,128)S(1)}, f32[48,3,96]{2,0,1:T(8,128)}, u32[]{:S(2)}) copy-start(f32[48,3,96]{2,0,1:T(8,128)} %param.44) | copy-start | bytes 165892
  265.8 196.7 %copy-start.12 = (f32[48,3,96]{2,0,1:T(8,128)S(1)}, f32[48,3,96]{2,0,1:T(8,128)}, u32[]{:S(2)}) copy-start(f32[48,3,96]{2,0,1:T(8,128)} %param.38) | copy-start | bytes 165892
  265.8 198.4 %copy-start.25 = (f32[48]{0:T(128)S(1)}, f32[48]{0:T(128)}, u32[]{:S(2)}) copy-start(f32[48]{0:T(128)} %param.37) | copy-start | bytes 580
  265.8 198.4 %copy-start.26 = (f32[48]{0:T(128)S(1)}, f32[48]{0:T(128)}, u32[]{:S(2)}) copy-start(f32[48]{0:T(128)} %param.49) | copy-start | bytes 580
  265.8 198.4 %copy-start.27 = (f32[48]{0:T(128)S(1)}, f32[48]{0:T(128)}, u32[]{:S(2)}) copy-start(f32[48]{0:T(128)} %param.43) | copy-start | bytes 580
  265.8 198.9 %copy-start.5 = (f32[384,48]{0,1:T(8,128)S(1)}, f32[384,48]{0,1:T(8,128)}, u32[]{:S(2)}) copy-start(f32[384,48]{0,1:T(8,128)} %param.35) | copy-start | bytes 221188
  265.9 198.9 %copy-start.13 = (f32[384,48]{0,1:T(8,128)S(1)}, f32[384,48]{0,1:T(8,128)}, u32[]{:S(2)}) copy-start(f32[384,48]{0,1:T(8,128)} %param.47) | copy-start | bytes 221188
  265.9 198.9 %copy-start.14 = (f32[384,48]{0,1:T(8,128)S(1)}, f32[384,48]{0,1:T(8,128)}, u32[]{:S(2)}) copy-start(f32[384,48]{0,1:T(8,128)} %param.41) | copy-start | bytes 221188
  265.9 200.5 %copy-start.6 = (f32[48,384]{1,0:T(8,128)S(1)}, f32[48,384]{1,0:T(8,128)}, u32[]{:S(2)}) copy-start(f32[48,384]{1,0:T(8,128)} %param.34) | copy-start | bytes 221188
  265.9 200.5 %copy-start.15 = (f32[48,384]{1,0:T(8,128)S(1)}, f32[48,384]{1,0:T(8,128)}, u32[]{:S(2)}) copy-start(f32[48,384]{1,0:T(8,128)} %param.46) | copy-start | bytes 221188
  265.9 200.4 %copy-start.16 = (f32[48,384]{1,0:T(8,128)S(1)}, f32[48,384]{1,0:T(8,128)}, u32[]{:S(2)}) copy-start(f32[48,384]{1,0:T(8,128)} %param.40) | copy-start | bytes 221188
  293.2 174.7 %copy-start.10 = (f32[96,48]{0,1:T(8,128)S(1)}, f32[96,48]{0,1:T(8,128)}, u32[]{:S(2)}) copy-start(f32[96,48]{0,1:T(8,128)} %param.33) | copy-start | bytes 55300
  293.2 174.7 %copy-start.18 = (f32[96,48]{0,1:T(8,128)S(1)}, f32[96,48]{0,1:T(8,128)}, u32[]{:S(2)}) copy-start(f32[96,48]{0,1:T(8,128)} %param.45) | copy-start | bytes 55300
  293.2 174.7 %copy-start.19 = (f32[96,48]{0,1:T(8,128)S(1)}, f32[96,48]{0,1:T(8,128)}, u32[]{:S(2)}) copy-start(f32[96,48]{0,1:T(8,128)} %param.39) | copy-start | bytes 55300
  (11 other events, 69.2 us)
Sparse Core Ops, SparseCore 0:
  49.0 34.0 all-gather.13
  155.1 68.9 reduce-scatter.2
  226.4 32.9 all-gather.15
  260.9 28.5 all-gather.11
  290.9 28.5 all-gather.7
  323.2 66.7 reduce-scatter.4
  392.1 27.4 all-gather.9
